TPU v7x, 32 devices: a whole 2x2x4 slice. The times are simulated.
32 devices in a mesh: groups: 2 (over y), sector: 4 (over z), op: 2 (over x), sub: 2 (over core).
Axes of the slice: x: 2, y: 2, z: 4, core: 2. Of those that a mesh axis runs over, the one named last changes fastest.
Arguments:
- wavefunction: bfloat16 [8, 4, 2, 128, 128], P(('groups', 'sector')), parts along dimension 0, may hold values from -6 to 6
- right_env: bfloat16 [32, 4, 128, 128], P(('groups', 'op', 'sub'), 'sector'), parts along dimension 0, may hold values from -0.5 to 0.5
- left_env: bfloat16 [32, 4, 128, 128], P(('groups', 'op', 'sub'), 'sector'), parts along dimension 0, may hold values from -0.5 to 0.5
- site_ops: float32 [32, 2, 2], P(('groups', 'op', 'sub')), parts along dimension 0, may hold values from -1 to 1
- right_map: int32 [32, 4], P(('groups', 'op', 'sub')), parts along dimension 0, may hold values from 0 to 3
- left_map: int32 [32, 4], P(('groups', 'op', 'sub')), parts along dimension 0, may hold values from 0 to 3
Outputs:
- sigma: bfloat16 [8, 4, 2, 128, 128], P(('groups', 'op', 'sub'), 'sector'), parts along dimension 0
There are 2 independent parts, one for each index of `groups`. A program takes and returns all parts, laid end to end along the dimension named above; each array names one. Nothing has to cross between parts.
All inputs are finite; a program needn't handle non-finite values.
Results may differ from a plain program's by a relative error of at most 0.0058.
Values may be sent and summed in bfloat16 or wider, within the bound.
A program may use at most 64 MiB of HBM per device.

v0:
```python
import jax
import jax.numpy as jnp
from jax import lax
from jax.sharding import PartitionSpec as P


def local(wavefunction, right_env, left_env, site_ops, right_map, left_map):
    highest = lax.Precision.HIGHEST
    term_count = right_env.shape[0]
    sectors = wavefunction.shape[1]
    sector_ids = jnp.arange(sectors, dtype=jnp.int32)
    right_full = lax.all_gather(right_env, "sector", axis=1, tiled=True)
    coupled_terms = []
    for term_index in range(term_count):
        images = jnp.einsum(
            "abpij,bjl->bapil",
            wavefunction,
            right_full[term_index],
            preferred_element_type=jnp.float32,
        )
        select = (right_map[term_index][:, None] == sector_ids[None, :]).astype(jnp.float32)
        routed = jnp.einsum("bc,bapil->acpil", select, images, precision=highest)
        coupled = jnp.einsum(
            "pq,acpil->acqil", site_ops[term_index], routed, precision=highest
        ).astype(jnp.bfloat16)
        coupled_terms.append(coupled)
    coupled_all = jnp.stack(coupled_terms, axis=0)
    source_select = (left_map[:, :, None] == sector_ids[None, None, :]).astype(jnp.bfloat16)
    local_products = jnp.einsum(
        "taim,tacqil->tacqml", left_env, coupled_all, preferred_element_type=jnp.float32
    ).astype(jnp.bfloat16)
    term_partial = jnp.einsum(
        "tad,tacqml->dcqml",
        source_select,
        lax.all_to_all(local_products, "sector", split_axis=2, concat_axis=1, tiled=True),
        preferred_element_type=jnp.float32,
    )
    reduced = lax.psum_scatter(term_partial, ("op", "sub"), scatter_dimension=0, tiled=True)
    return reduced.astype(jnp.bfloat16)


def solution(mesh):
    in_specs = (
        P(("groups", "sector"), None, None, None, None),
        P(("groups", "op", "sub"), "sector", None, None),
        P(("groups", "op", "sub"), "sector", None, None),
        P(("groups", "op", "sub"), None, None),
        P(("groups", "op", "sub"), None),
        P(("groups", "op", "sub"), None),
    )
    out_specs = P(("groups", "op", "sub"), "sector", None, None, None)
    return jax.shard_map(local, mesh=mesh, in_specs=in_specs, out_specs=out_specs, check_vma=False)
```

profile of v0, /device:TPU:0, one launch (start us, length us, event | category | flops | bytes accessed | tf_op | source)
XLA Modules:
  0.0 101.6 jit_solution(7467542836849557754)
XLA Ops:
  6.5 0.0 copy-start
  6.5 17.7 %all_gather.3 = bf16[4,4,128,128]{3,2,1,0:T(8,128)(2,1)S(1)} all-gather(bf16[4,1,128,128]{3,2,1,0:T(8,128)(2,1)} %param.7), channel_id=1, replica_groups=mesh['groups'=2,'sector'=4,'op'=2,'sub'=2] {'sector'}, dimensions={1}, use_global_device_ids=true | all-gather | bytes 655360 | tf_op jit(solution)/shard_map/all_gather | solution.py:12
  24.2 0.0 copy-done
  24.2 0.2 fusion.21
  24.5 0.2 fusion.19
  24.7 0.0 copy-start.3
  24.7 0.0 copy-start.2
  24.7 0.2 fusion.17
  24.9 0.2 fusion.15
  25.1 0.2 copy-done.3
  25.4 0.0 copy-done.2
  25.4 0.1 fusion.43
  25.4 0.1 copy.63
  25.5 0.1 copy.64
  25.6 0.1 copy.65
  25.7 0.1 copy.66
  25.8 0.9 convolution_bitcast_fusion.4
  26.7 2.1 %fusion.1 = bf16[1,1,4,2,128,128]{5,3,4,2,1,0:T(2,128)(2,1)S(1)} fusion(f32[4,2,128,128]{3,0,2,1:T(4,128)S(1)} %convolution_bitcast_fusion.4, f32[1,2,2]{1,2,0:T(2,128)S(1)} %copy.63), kind=kOutput, calls=%fused_computation.11 | convolution fusion | flops 3276800 | bytes 786448 | tf_op jit(solution)/shard_map/pq,acpil->acqil/dot_general | solution.py:23
  28.8 0.9 convolution_bitcast_fusion.3
  29.7 2.1 %fusion.2 = bf16[1,1,4,2,128,128]{5,3,4,2,1,0:T(2,128)(2,1)S(1)} fusion(f32[4,2,128,128]{3,0,2,1:T(4,128)S(1)} %convolution_bitcast_fusion.3, f32[1,2,2]{1,2,0:T(2,128)S(1)} %copy.64), kind=kOutput, calls=%fused_computation.12 | convolution fusion | flops 3276800 | bytes 786448 | tf_op jit(solution)/shard_map/pq,acpil->acqil/dot_general | solution.py:23
  31.8 0.9 convolution_bitcast_fusion.2
  32.7 2.1 %fusion.3 = bf16[1,1,4,2,128,128]{5,3,4,2,1,0:T(2,128)(2,1)S(1)} fusion(f32[4,2,128,128]{3,0,2,1:T(4,128)S(1)} %convolution_bitcast_fusion.2, f32[1,2,2]{1,2,0:T(2,128)S(1)} %copy.65), kind=kOutput, calls=%fused_computation.13 | convolution fusion | flops 3276800 | bytes 786448 | tf_op jit(solution)/shard_map/pq,acpil->acqil/dot_general | solution.py:23
  34.7 0.9 convolution_bitcast_fusion.1
  35.6 2.3 %fusion.4 = bf16[1,1,4,2,128,128]{5,3,4,2,1,0:T(2,128)(2,1)S(1)} fusion(f32[4,2,128,128]{3,0,2,1:T(4,128)S(1)} %convolution_bitcast_fusion.1, f32[1,2,2]{1,2,0:T(2,128)S(1)} %copy.66), kind=kOutput, calls=%fused_computation.14 | convolution fusion | flops 3276800 | bytes 786448 | tf_op jit(solution)/shard_map/pq,acpil->acqil/dot_general | solution.py:23
  37.9 0.0 copy-start.1
  37.9 2.0 %maximum_bitcast_fusion = bf16[4,4,2,128,128]{4,2,3,1,0:T(2,128)(2,1)S(1)} fusion(bf16[1,1,4,2,128,128]{5,3,4,2,1,0:T(2,128)(2,1)S(1)} %fusion.4, bf16[1,1,4,2,128,128]{5,3,4,2,1,0:T(2,128)(2,1)S(1)} %fusion.3, bf16[1,1,4,2,128,128]{5,3,4,2,1,0:T(2,128)(2,1)S(1)} %fusion.2, bf16[1,1,4,2,128,128]{5,3,4,2,1,0:T(2,128)(2,1)S(1)} %fusion.1), kind=kLoop, calls=%fused_computation.15 | loop fusion | flops 1572864 | bytes 2097152 | tf_op jit(solution)/shard_map/reshape.24
  39.9 0.0 copy-done.1
  39.9 0.5 fusion
  40.4 1.1 %copy.45 = bf16[4,1,4,2,128,128]{4,5,3,0,1,2:T(8,128)(2,1)} copy(bf16[4,1,4,2,128,128]{4,5,3,2,0,1:T(8,128)(2,1)S(1)} %fusion) | data formatting | bytes 2097152 | tf_op jit(solution)/shard_map/convert_element_type | solution.py:31
  41.5 0.0 copy-start.4
  41.5 5.5 %all-to-all-start = ((bf16[4,1,4,2,128,128]{4,5,3,0,1,2:T(8,128)(2,1)}), bf16[4,1,4,2,128,128]{4,5,3,0,1,2:T(8,128)(2,1)S(1)}, u32[]{:S(2)}, u32[]{:S(2)}) async-start(bf16[4,1,4,2,128,128]{4,5,3,0,1,2:T(8,128)(2,1)} %copy.45), calls=%async_computation | async-start | bytes 2097152 | tf_op jit(solution)/shard_map/all_to_all | solution.py:35
  47.0 0.0 reduce-scatter.2.cloned.1.call-start
  47.0 0.0 copy-done.4
  47.0 0.1 copy.31
  47.1 22.6 %all-to-all-done = bf16[4,1,4,2,128,128]{4,5,3,0,1,2:T(8,128)(2,1)S(1)} async-done(((bf16[4,1,4,2,128,128]{4,5,3,0,1,2:T(8,128)(2,1)}), bf16[4,1,4,2,128,128]{4,5,3,0,1,2:T(8,128)(2,1)S(1)}, u32[]{:S(2)}, u32[]{:S(2)}) %all-to-all-start) | async-done | bytes 1048608 | tf_op jit(solution)/shard_map/all_to_all | solution.py:35
  69.7 1.0 copy.46
  70.6 0.8 convolution_bitcast_fusion
  71.5 0.8 copy.47
  72.3 0.0 reduce-scatter.2.cloned.1.call-update
  72.3 20.9 %reduce-scatter.2.cloned.1.call-done = f32[1,1,2,128,128]{4,3,2,1,0:T(8,128)} async-done(((f32[4,1,2,128,128]{4,3,2,1,0:T(8,128)}), f32[1,1,2,128,128]{4,3,2,1,0:T(8,128)}) %reduce-scatter.2.cloned.1.call-update) | async-done | bytes 131088 | tf_op jit(solution)/shard_map/reduce_scatter | solution.py:38
  93.2 1.5 %convert_element_type.68 = bf16[1,1,2,128,128]{4,3,2,1,0:T(8,128)(2,1)} convert(f32[1,1,2,128,128]{4,3,2,1,0:T(8,128)} %reduce-scatter.2.cloned.1.call-done) | non-fusion elementwise | flops 32768 | bytes 196608 | tf_op jit(solution)/shard_map/convert_element_type | solution.py:39
  (1 shorter events, 0.0 us)
Async XLA Ops:
  6.5 17.7 %copy-start = (bf16[1,4,2,128,128]{4,3,2,1,0:T(8,128)(2,1)S(1)}, bf16[1,4,2,128,128]{4,3,2,1,0:T(8,128)(2,1)}, u32[]{:S(2)}) copy-start(bf16[1,4,2,128,128]{4,3,2,1,0:T(8,128)(2,1)} %param.6) | copy-start | bytes 786436
  24.7 0.7 copy-start.3
  24.7 0.7 copy-start.2
  37.9 2.0 %copy-start.1 = (bf16[4,1,128,128]{3,2,1,0:T(8,128)(2,1)S(1)}, bf16[4,1,128,128]{3,2,1,0:T(8,128)(2,1)}, u32[]{:S(2)}) copy-start(bf16[4,1,128,128]{3,2,1,0:T(8,128)(2,1)} %param.8) | copy-start | bytes 393220
  41.5 5.5 %copy-start.4 = (s32[4,4]{1,0:T(4,128)S(1)}, s32[4,4]{1,0:T(4,128)}, u32[]{:S(2)}) copy-start(s32[4,4]{1,0:T(4,128)} %param.11) | copy-start | bytes 196
  41.5 28.2 %all-to-all-start = ((bf16[4,1,4,2,128,128]{4,5,3,0,1,2:T(8,128)(2,1)}), bf16[4,1,4,2,128,128]{4,5,3,0,1,2:T(8,128)(2,1)S(1)}, u32[]{:S(2)}, u32[]{:S(2)}) async-start(bf16[4,1,4,2,128,128]{4,5,3,0,1,2:T(8,128)(2,1)} %copy.45), calls=%async_computation | async-start | bytes 2097152 | tf_op jit(solution)/shard_map/all_to_all | solution.py:35
  47.0 46.2 %reduce-scatter.2.cloned.1.call-start = ((), (), s32[]{:S(2)}) async-start(), calls=%async_computation.2 | async-start | bytes 655360 | tf_op jit(solution)/shard_map/reduce_scatter | solution.py:38
Sparse Core Ops, SparseCore 0:
  72.4 20.7 reduce-scatter.1
where the time goes:
time: 102 us
  waiting for transfers between devices  43.5 us (43%)
  blocking collectives  17.7 us (17%)
  matrix products  14.2 us (14%)
  between operations  13.5 us (13%)
  starting transfers between devices  5.51 us (5%)
  local copies, waits for them, and re-layouts  3.68 us (4%)
  other arithmetic  3.5 us (3%)
    all_to_all x1, waiting for transfers between devices, local(): lax.all_to_all(local_products, 'sector', split_axis=2, concat_axis=1, til...  22.6 us
    reduce_scatter x1, waiting for transfers between devices, local(): lax.psum_scatter(term_partial, ('op', 'sub'), scatter_dimension=0, tiled=...  20.9 us
    all_gather x1, blocking collectives, local(): right_full = lax.all_gather(right_env, 'sector', axis=1, tiled=True)  17.7 us
    dot_general x4, matrix products, local(): jnp.einsum('pq,acpil->acqil', site_ops[term_index], routed, precision=hig...  8.41 us
    all_to_all x1, starting transfers between devices, local(): lax.all_to_all(local_products, 'sector', split_axis=2, concat_axis=1, til...  5.51 us
    dot_general x4, matrix products, local(): routed = jnp.einsum('bc,bapil->acpil', select, images, precision=highest)  3.56 us
  transfers between devices with their start and end apart: 2, of which 2 were waited for; matrix products, arithmetic and copies ran while one was open for 0% of the time, Pallas kernels for 0%

commit v1 on v0

--- a/solution.py
+++ b/solution.py
@@ -1,10 +1,19 @@
+import functools
+
 import jax
 import jax.numpy as jnp
 from jax import lax
+from jax.experimental import pallas as pl
+from jax.experimental.pallas import tpu as pltpu
 from jax.sharding import PartitionSpec as P
 
-
-def local(wavefunction, right_env, left_env, site_ops, right_map, left_map):
+MESH = pl.DeviceIdType.MESH
+BF16 = jnp.bfloat16
+F32 = jnp.float32
+PARTS = 1
+
+
+def routed_plan(wavefunction, right_env, left_env, site_ops, right_map, left_map):
     highest = lax.Precision.HIGHEST
     term_count = right_env.shape[0]
     sectors = wavefunction.shape[1]
@@ -39,7 +48,289 @@
     return reduced.astype(jnp.bfloat16)
 
 
+def fused_kernel(Z, O, U, K, D, Q, N, H, order, psi_ref, r_ref, l_ref, tab_ref, out_ref, stage, rbuf, lbuf, tabs, lm, mask, cp, pf, psend, prcv, fin,
+                 t_send, t_recv, up_send, dn_send, l_send, l_recv, tab_send, tab_recv, p_send, p_recv, f_send, f_recv):
+    T = O * U
+    W = N // T
+    LH = W // H
+    z = lax.axis_index("sector")
+    o = lax.axis_index("op")
+    u = lax.axis_index("sub")
+    t = o * U + u
+    peers = []
+    for i in range(O):
+        for j in range(U):
+            if i or j:
+                po, pu = lax.rem(o + i, O), lax.rem(u + j, U)
+                peers.append((i * U + j, po * U + pu, {"op": po, "sub": pu}))
+    zpeers = [(r, lax.rem(z + r, Z)) for r in range(1, Z)]
+
+    barrier = pltpu.get_barrier_semaphore()
+    for e, pt, dev in peers:
+        pl.semaphore_signal(barrier, inc=1, device_id=dev, device_id_type=MESH)
+    for r, pz in zpeers:
+        pl.semaphore_signal(barrier, inc=1, device_id={"sector": pz}, device_id_type=MESH)
+
+    for k in range(K):
+        turned = r_ref[k, 0].astype(F32).T.astype(BF16)
+        for tt in range(T):
+            for h in range(H):
+                at = tt * W + h * LH
+                stage[tt, h, k] = turned[at:at + LH]
+    for h in range(H):
+        rbuf[z, h, 0] = stage[t, h]
+
+    pl.semaphore_wait(barrier, len(peers) + len(zpeers))
+
+    def rcopy(e, pt, dev, h):
+        return pltpu.make_async_remote_copy(
+            src_ref=stage.at[pt, h], dst_ref=rbuf.at[z, h, e],
+            send_sem=t_send.at[h, e], recv_sem=t_recv.at[z, h, e], device_id=dev, device_id_type=MESH)
+
+    def tcopy(e, pt, dev):
+        return pltpu.make_async_remote_copy(
+            src_ref=tab_ref, dst_ref=tabs.at[e - 1],
+            send_sem=tab_send.at[e - 1], recv_sem=tab_recv.at[e - 1], device_id=dev, device_id_type=MESH)
+
+    def lcopy(e, pt, dev):
+        return pltpu.make_async_remote_copy(
+            src_ref=l_ref, dst_ref=lbuf.at[e - 1],
+            send_sem=l_send.at[e - 1], recv_sem=l_recv.at[e - 1], device_id=dev, device_id_type=MESH)
+
+    def up(b, h, e):
+        return pltpu.make_async_remote_copy(
+            src_ref=rbuf.at[b, h, e], dst_ref=rbuf.at[b, h, e],
+            send_sem=up_send.at[b, h, e], recv_sem=t_recv.at[b, h, e], device_id={"sector": z + 1}, device_id_type=MESH)
+
+    def down(b, h, e):
+        return pltpu.make_async_remote_copy(
+            src_ref=rbuf.at[b, h, e], dst_ref=rbuf.at[b, h, e],
+            send_sem=dn_send.at[b, h, e], recv_sem=t_recv.at[b, h, e], device_id={"sector": z - 1}, device_id_type=MESH)
+
+    def pcopy(h, r, pz):
+        return pltpu.make_async_remote_copy(
+            src_ref=psend.at[h, pz], dst_ref=prcv.at[h, z],
+            send_sem=p_send.at[h, r - 1], recv_sem=p_recv.at[h, z], device_id={"sector": pz}, device_id_type=MESH)
+
+    def fcopy(h, e, pt, dev):
+        return pltpu.make_async_remote_copy(
+            src_ref=fin.at[h, pt], dst_ref=out_ref.at[t, h],
+            send_sem=f_send.at[h, e - 1], recv_sem=f_recv.at[h, e - 1], device_id=dev, device_id_type=MESH)
+
+    for h in range(H):
+        for e, pt, dev in peers:
+            rcopy(e, pt, dev, h).start()
+        if h == 0:
+            for e, pt, dev in peers:
+                tcopy(e, pt, dev).start()
+    for e, pt, dev in peers:
+        lcopy(e, pt, dev).start()
+
+    def gather(h, r):
+        if r == 0:
+            for e in range(T):
+                if e:
+                    up(z, h, e).wait_recv()
+
+                @pl.when(z < Z - 1)
+                def _():
+                    up(z, h, e).start()
+
+                @pl.when(z > 0)
+                def _():
+                    down(z, h, e).start()
+            return
+        for e in range(T):
+            @pl.when(z - r >= 0)
+            def _():
+                up(z - r, h, e).wait_recv()
+
+                @pl.when(z < Z - 1)
+                def _():
+                    up(z - r, h, e).start()
+
+            @pl.when(z + r <= Z - 1)
+            def _():
+                down(z + r, h, e).wait_recv()
+
+                @pl.when(z > 0)
+                def _():
+                    down(z + r, h, e).start()
+
+    def table(e):
+        return tab_ref[...] if e == 0 else tabs[e - 1]
+
+    def row(tab, at):
+        return jnp.broadcast_to(tab[:, at:at + 1], (tab.shape[0], N))
+
+    def prepare():
+        for e, pt, dev in peers:
+            tcopy(e, pt, dev).wait_recv()
+        for e in range(T):
+            tab = table(e)
+            for b in range(D):
+                want = row(tab, b)
+                for c in range(D):
+                    hit = jnp.where(want == float(c), 1.0, 0.0)
+                    for k in range(K):
+                        mask[c, (e * K + k) * LH:(e * K + k + 1) * LH, b * N:(b + 1) * N] = jnp.broadcast_to(hit[k:k + 1], (LH, N)).astype(BF16)
+
+    def prepare_left():
+        for e, pt, dev in peers:
+            lcopy(e, pt, dev).wait_recv()
+        for e in range(T):
+            want = row(table(e), D)
+            for d in range(D):
+                hit = jnp.where(want == float(d), 1.0, 0.0)
+                for k in range(K):
+                    block = l_ref[k, 0] if e == 0 else lbuf[e - 1, k, 0]
+                    lm[(e * K + k) * N:(e * K + k + 1) * N, d * N:(d + 1) * N] = block * jnp.broadcast_to(hit[k:k + 1], (N, N)).astype(BF16)
+
+    def compute(h):
+        rows = T * K * LH
+        right = jnp.concatenate([rbuf[b, h].reshape(rows, N) for b in range(D)], axis=1)
+        for c in range(D):
+            masked = right * mask[c]
+            routed = None
+            for b in range(D):
+                part = lax.dot_general(masked[:, b * N:(b + 1) * N], psi_ref[0, b].reshape(Q * N, N),
+                                       (((1,), (1,)), ((), ())), preferred_element_type=F32)
+                routed = part if routed is None else routed + part
+            for e in range(T):
+                tab = table(e)
+                for k in range(K):
+                    at = (e * K + k) * LH
+                    for q in range(Q):
+                        coupled = None
+                        for p in range(Q):
+                            weight = row(tab, D + 1 + p * Q + q)[k:k + 1]
+                            part = routed[at:at + LH, p * N:(p + 1) * N] * weight
+                            coupled = part if coupled is None else coupled + part
+                        cp[(c * Q + q) * LH:(c * Q + q + 1) * LH, (e * K + k) * N:(e * K + k + 1) * N] = coupled.astype(BF16)
+
+    def products(h):
+        sums = jnp.dot(cp[...], lm[...], preferred_element_type=F32)
+        for c in range(D):
+            part = sums[c * Q * LH:(c + 1) * Q * LH]
+            pf[h, c] = part
+            psend[h, c] = part.astype(BF16)
+        for r, pz in zpeers[::-1]:
+            pcopy(h, r, pz).start()
+
+    def finish(h):
+        total = pf[h, z]
+        for r, pz in zpeers:
+            pltpu.make_async_remote_copy(
+                src_ref=psend.at[h, pz], dst_ref=prcv.at[h, pz], send_sem=p_send.at[h, r - 1],
+                recv_sem=p_recv.at[h, pz], device_id={"sector": pz}, device_id_type=MESH).wait_recv()
+            total = total + prcv[h, pz].astype(F32)
+        total = total.astype(BF16)
+        for d in range(D):
+            fin[h, d] = total[:, d * N:(d + 1) * N].reshape(Q, LH, N)
+        for e, pt, dev in peers:
+            fcopy(h, e, pt, dev).start()
+        out_ref[t, h] = fin[h, t]
+
+    for step in order:
+        kind = step[0]
+        if kind == "gather":
+            gather(step[1], step[2])
+        elif kind == "prepare":
+            prepare()
+        elif kind == "left":
+            prepare_left()
+        elif kind == "compute":
+            compute(step[1])
+        elif kind == "products":
+            products(step[1])
+        else:
+            finish(step[1])
+
+    for h in range(H):
+        for e, pt, dev in peers:
+            fcopy(h, e, pt, dev).wait_recv()
+            fcopy(h, e, pt, dev).wait_send()
+            rcopy(e, pt, dev, h).wait_send()
+        for r, pz in zpeers:
+            pcopy(h, r, pz).wait_send()
+        for e in range(T):
+            for r in range(Z):
+                @pl.when(jnp.logical_and(z - r >= 0, z < Z - 1))
+                def _():
+                    up(z - r, h, e).wait_send()
+
+                @pl.when(jnp.logical_and(z + r <= Z - 1, z > 0))
+                def _():
+                    down(z + r, h, e).wait_send()
+    for e, pt, dev in peers:
+        tcopy(e, pt, dev).wait_send()
+        lcopy(e, pt, dev).wait_send()
+
+
+def steps(Z, H):
+    if H == 1:
+        order = [("gather", 0, 0), ("prepare",)]
+        order += [("gather", 0, r) for r in range(1, Z - 1)]
+        order += [("left",), ("gather", 0, Z - 1), ("compute", 0), ("products", 0), ("finish", 0)]
+        return order
+    order = [("gather", 0, 0), ("prepare",), ("gather", 0, 1), ("gather", 0, 2), ("gather", 1, 0), ("left",)]
+    order += [("gather", 0, 3), ("gather", 1, 1), ("compute", 0), ("products", 0), ("gather", 1, 2)]
+    order += [("gather", 1, 3), ("compute", 1), ("products", 1), ("finish", 0), ("finish", 1)]
+    return order
+
+
+def fused_plan(Z, O, U, wavefunction, right_env, left_env, site_ops, right_map, left_map):
+    K = right_env.shape[0]
+    _, D, Q, N, _ = wavefunction.shape
+    T, H = O * U, PARTS
+    LH = N // T // H
+    own = lax.axis_index("sector")
+    left = lax.dynamic_slice_in_dim(left_map, own, 1, axis=1)
+    tab = jnp.concatenate([right_map.astype(F32), left.astype(F32), site_ops.reshape(K, Q * Q)], axis=1)
+    tab = jnp.pad(tab, ((0, -K % 8), (0, 128 - tab.shape[1])))
+    dma = pltpu.SemaphoreType.DMA
+    vmem = pl.BlockSpec(memory_space=pltpu.VMEM)
+    out = pl.pallas_call(
+        functools.partial(fused_kernel, Z, O, U, K, D, Q, N, H, steps(Z, H)),
+        out_shape=jax.ShapeDtypeStruct((T, H, Q, LH, N), BF16),
+        in_specs=[vmem] * 4,
+        out_specs=vmem,
+        scratch_shapes=[
+            pltpu.VMEM((T, H, K, LH, N), BF16),
+            pltpu.VMEM((D, H, T, K, LH, N), BF16),
+            pltpu.VMEM((T - 1,) + left_env.shape, BF16),
+            pltpu.VMEM((T - 1,) + tab.shape, F32),
+            pltpu.VMEM((T * K * N, D * N), BF16),
+            pltpu.VMEM((D, T * K * LH, D * N), BF16),
+            pltpu.VMEM((D * Q * LH, T * K * N), BF16),
+            pltpu.VMEM((H, D, Q * LH, D * N), F32),
+            pltpu.VMEM((H, D, Q * LH, D * N), BF16),
+            pltpu.VMEM((H, D, Q * LH, D * N), BF16),
+            pltpu.VMEM((H, D, Q, LH, N), BF16),
+            dma((H, T)), dma((D, H, T)), dma((D, H, T)), dma((D, H, T)),
+            dma((T - 1,)), dma((T - 1,)), dma((T - 1,)), dma((T - 1,)),
+            dma((H, Z - 1)), dma((H, Z)), dma((H, T - 1)), dma((H, T - 1)),
+        ],
+        compiler_params=pltpu.CompilerParams(collective_id=0, has_side_effects=True, vmem_limit_bytes=40 << 20),
+        name="sigma",
+    )(wavefunction, right_env, left_env, tab)
+    out = out.transpose(2, 4, 0, 1, 3).reshape(1, 1, Q, N, N)
+    return out
+
+
 def solution(mesh):
+    shape = mesh.shape
+    Z, O, U = shape["sector"], shape["op"], shape["sub"]
+
+    def local(wavefunction, right_env, left_env, site_ops, right_map, left_map):
+        K = right_env.shape[0]
+        a, D, Q, N, _ = wavefunction.shape
+        T = O * U
+        small = T * K * D * N * N * 2 <= (8 << 20)
+        if small and a == 1 and D == Z and D == T and N % (16 * T * PARTS) == 0 and N == 128:
+            return fused_plan(Z, O, U, wavefunction, right_env, left_env, site_ops, right_map, left_map)
+        return routed_plan(wavefunction, right_env, left_env, site_ops, right_map, left_map)
+
     in_specs = (
         P(("groups", "sector"), None, None, None, None),
         P(("groups", "op", "sub"), "sector", None, None),

time: 102 us -> 34.8 us (0.34)
  waiting for transfers between devices: 43.5 us -> 0 us
  Pallas kernels: 0 us -> 28.9 us
  blocking collectives: 17.7 us -> 0 us
  matrix products: 14.2 us -> 0 us
  between operations: 13.5 us -> 0.03 us
  starting transfers between devices: 5.51 us -> 0 us
  other arithmetic: 3.5 us -> 0.15 us
  local copies, waits for them, and re-layouts: 3.68 us -> 5.48 us
    pallas_call x0 -> x1, Pallas kernels: none -> 28.9 us  [fused_plan(): pl.pallas_call(functools.partial(fused_kernel, Z, O, U, K, D, Q, N, H, st...]
    all_to_all x1 -> x0, waiting for transfers between devices: 22.6 us -> none  [local(): lax.all_to_all(local_products, 'sector', split_axis=2, concat_axis=1, til...]
    reduce_scatter x1 -> x0, waiting for transfers between devices: 20.9 us -> none  [local(): lax.psum_scatter(term_partial, ('op', 'sub'), scatter_dimension=0, tiled=...]
    all_gather x1 -> x0, blocking collectives: 17.7 us -> none  [local(): right_full = lax.all_gather(right_env, 'sector', axis=1, tiled=True)]
    dot_general x14 -> x0, matrix products: 14.2 us -> none  [the longest x4 8.41 us: local(): jnp.einsum('pq,acpil->acqil', site_ops[term_index], routed, precision=hig...]
    all_to_all x1 -> x0, starting transfers between devices: 5.51 us -> none  [local(): lax.all_to_all(local_products, 'sector', split_axis=2, concat_axis=1, til...]
    unnamed x11 -> x12, local copies, waits for them, and re-layouts: 0.34 us -> 4.64 us
    another operation x1 -> x0, other arithmetic: 1.96 us -> none
  transfers between devices with their start and end apart: 2 -> 0, of which waited for: 2 -> 0; matrix products, arithmetic and copies ran while one was open for 0% -> 0% of each run, Pallas kernels for 0% -> 0%
where the time goes in v1:
time: 34.8 us; the launch traced here: 34.5 us
  Pallas kernels  28.9 us (83%)
  local copies, waits for them, and re-layouts  5.48 us (16%)
    pallas_call x1, Pallas kernels, fused_plan(): pl.pallas_call(functools.partial(fused_kernel, Z, O, U, K, D, Q, N, H, st...  28.9 us
    unnamed x12, local copies, waits for them, and re-layouts  4.64 us
    reshape x1, local copies, waits for them, and re-layouts, fused_plan(): out = out.transpose(2, 4, 0, 1, 3).reshape(1, 1, Q, N, N)  0.74 us

profile of v1, /device:TPU:0, one launch (start us, length us, event | category | flops | bytes accessed | tf_op | source)
XLA Modules:
  0.0 34.5 jit_solution(15796692645131692151)
XLA Ops:
  0.0 0.0 copy-start.3
  0.0 0.7 %copy-done.3 = s32[4,4]{1,0:T(4,128)S(1)} copy-done((s32[4,4]{1,0:T(4,128)S(1)}, s32[4,4]{1,0:T(4,128)}, u32[]{:S(2)}) %copy-start.3) | copy-done | bytes 88
  0.7 0.0 copy-start.4
  0.7 0.1 dynamic-slice_convert_fusion
  0.8 0.6 %copy-done.4 = f32[4,2,2]{0,2,1:T(2,128)S(1)} copy-done((f32[4,2,2]{0,2,1:T(2,128)S(1)}, f32[4,2,2]{0,2,1:T(2,128)}, u32[]{:S(2)}) %copy-start.4) | copy-done | bytes 88
  1.4 0.0 copy-start.5
  1.4 0.1 copy.8
  1.5 0.6 %copy-done.5 = s32[4,4]{1,0:T(4,128)S(1)} copy-done((s32[4,4]{1,0:T(4,128)S(1)}, s32[4,4]{1,0:T(4,128)}, u32[]{:S(2)}) %copy-start.5) | copy-done | bytes 88
  2.0 0.1 select_maximum_fusion.tab_ref
  2.1 0.0 copy-start
  2.1 0.9 %copy-done = bf16[1,4,2,128,128]{4,3,2,1,0:T(8,128)(2,1)S(1)} copy-done((bf16[1,4,2,128,128]{4,3,2,1,0:T(8,128)(2,1)S(1)}, bf16[1,4,2,128,128]{4,3,2,1,0:T(8,128)(2,1)}, u32[]{:S(2)}) %copy-start) | copy-done | bytes 262168
  3.1 0.0 copy-start.1
  3.1 0.9 %copy-done.1 = bf16[4,1,128,128]{3,2,1,0:T(8,128)(2,1)S(1)} copy-done((bf16[4,1,128,128]{3,2,1,0:T(8,128)(2,1)S(1)}, bf16[4,1,128,128]{3,2,1,0:T(8,128)(2,1)}, u32[]{:S(2)}) %copy-start.1) | copy-done | bytes 131096
  4.0 0.0 copy-start.2
  4.0 0.9 %copy-done.2 = bf16[4,1,128,128]{3,2,1,0:T(8,128)(2,1)S(1)} copy-done((bf16[4,1,128,128]{3,2,1,0:T(8,128)(2,1)S(1)}, bf16[4,1,128,128]{3,2,1,0:T(8,128)(2,1)}, u32[]{:S(2)}) %copy-start.2) | copy-done | bytes 131096
  4.9 28.9 %sigma.1 = bf16[4,1,2,32,128]{4,3,2,1,0:T(8,128)(2,1)S(1)} custom-call(bf16[1,4,2,128,128]{4,3,2,1,0:T(8,128)(2,1)S(1)} %copy-done, bf16[4,1,128,128]{3,2,1,0:T(8,128)(2,1)S(1)} %copy-done.1, bf16[4,1,128,128]{3,2,1,0:T(8,128)(2,1)S(1)} %copy-done.2, f32[8,128]{1,0:T(8,128)S(1)} %select_maximum_fusion.tab_ref), custom_call_target="tpu_custom_call" | custom-call | tf_op jit(solution)/shard_map/sigma/pallas_call | solution.py:293
  33.8 0.7 %copy.10 = bf16[1,1,2,128,128]{4,3,2,1,0:T(8,128)(2,1)} copy(bf16[1,1,2,128,128]{3,4,2,1,0:T(8,128)(2,1)S(1)} %bitcast.4) | data formatting | bytes 131072 | tf_op jit(solution)/shard_map/reshape | solution.py:317
  (2 shorter events, 0.0 us)
Async XLA Ops:
  0.0 0.7 %copy-start.3 = (s32[4,4]{1,0:T(4,128)S(1)}, s32[4,4]{1,0:T(4,128)}, u32[]{:S(2)}) copy-start(s32[4,4]{1,0:T(4,128)} %param.11) | copy-start | bytes 196
  0.7 0.7 %copy-start.4 = (f32[4,2,2]{0,2,1:T(2,128)S(1)}, f32[4,2,2]{0,2,1:T(2,128)}, u32[]{:S(2)}) copy-start(f32[4,2,2]{0,2,1:T(2,128)} %param.9) | copy-start | bytes 196
  1.4 0.7 %copy-start.5 = (s32[4,4]{1,0:T(4,128)S(1)}, s32[4,4]{1,0:T(4,128)}, u32[]{:S(2)}) copy-start(s32[4,4]{1,0:T(4,128)} %param.10) | copy-start | bytes 196
  2.1 1.0 %copy-start = (bf16[1,4,2,128,128]{4,3,2,1,0:T(8,128)(2,1)S(1)}, bf16[1,4,2,128,128]{4,3,2,1,0:T(8,128)(2,1)}, u32[]{:S(2)}) copy-start(bf16[1,4,2,128,128]{4,3,2,1,0:T(8,128)(2,1)} %psi_ref.1) | copy-start | bytes 786436
  3.1 0.9 %copy-start.1 = (bf16[4,1,128,128]{3,2,1,0:T(8,128)(2,1)S(1)}, bf16[4,1,128,128]{3,2,1,0:T(8,128)(2,1)}, u32[]{:S(2)}) copy-start(bf16[4,1,128,128]{3,2,1,0:T(8,128)(2,1)} %r_ref.1) | copy-start | bytes 393220
  4.0 0.9 %copy-start.2 = (bf16[4,1,128,128]{3,2,1,0:T(8,128)(2,1)S(1)}, bf16[4,1,128,128]{3,2,1,0:T(8,128)(2,1)}, u32[]{:S(2)}) copy-start(bf16[4,1,128,128]{3,2,1,0:T(8,128)(2,1)} %l_ref.1) | copy-start | bytes 393220

commit v2 on v1

--- a/solution.py
+++ b/solution.py
@@ -48,8 +48,8 @@
     return reduced.astype(jnp.bfloat16)
 
 
-def fused_kernel(Z, O, U, K, D, Q, N, H, order, psi_ref, r_ref, l_ref, tab_ref, out_ref, stage, rbuf, lbuf, tabs, lm, mask, cp, pf, psend, prcv, fin,
-                 t_send, t_recv, up_send, dn_send, l_send, l_recv, tab_send, tab_recv, p_send, p_recv, f_send, f_recv):
+def fused_kernel(Z, O, U, K, D, Q, N, H, order, psi_hbm, r_hbm, l_hbm, s_hbm, rm_hbm, lm_hbm, out_ref, psi_ref, r_ref, l_ref, s_ref, rm_ref, lm_ref, tab_ref, stage, rbuf, lbuf, tabs, lm, mask, cp, pf, psend, prcv, fin,
+                 in_sem, t_send, t_recv, up_send, dn_send, l_send, l_recv, tab_send, tab_recv, p_send, p_recv, f_send, f_recv):
     T = O * U
     W = N // T
     LH = W // H
@@ -65,12 +65,22 @@
                 peers.append((i * U + j, po * U + pu, {"op": po, "sub": pu}))
     zpeers = [(r, lax.rem(z + r, Z)) for r in range(1, Z)]
 
+    r_in = pltpu.make_async_copy(r_hbm, r_ref, in_sem.at[0])
+    l_in = pltpu.make_async_copy(l_hbm, l_ref, in_sem.at[1])
+    psi_in = pltpu.make_async_copy(psi_hbm, psi_ref, in_sem.at[2])
+    s_in = pltpu.make_async_copy(s_hbm, s_ref, in_sem.at[3])
+    rm_in = pltpu.make_async_copy(rm_hbm, rm_ref, in_sem.at[4])
+    lm_in = pltpu.make_async_copy(lm_hbm, lm_ref, in_sem.at[5])
+    for copy in (r_in, s_in, rm_in, lm_in, l_in, psi_in):
+        copy.start()
+
     barrier = pltpu.get_barrier_semaphore()
     for e, pt, dev in peers:
         pl.semaphore_signal(barrier, inc=1, device_id=dev, device_id_type=MESH)
     for r, pz in zpeers:
         pl.semaphore_signal(barrier, inc=1, device_id={"sector": pz}, device_id_type=MESH)
 
+    r_in.wait()
     for k in range(K):
         turned = r_ref[k, 0].astype(F32).T.astype(BF16)
         for tt in range(T):
@@ -80,6 +90,16 @@
     for h in range(H):
         rbuf[z, h, 0] = stage[t, h]
 
+    for copy in (s_in, rm_in, lm_in):
+        copy.wait()
+    tab_ref[...] = jnp.zeros_like(tab_ref)
+    tab_ref[0:K, 0:D] = rm_ref[...].astype(F32)
+    moved = lm_ref[...].astype(F32)
+    column = lax.broadcasted_iota(jnp.int32, (K, D), 1)
+    tab_ref[0:K, D:D + 1] = jnp.sum(jnp.where(column == z, moved, 0.0), axis=1, keepdims=True)
+    for p in range(Q):
+        tab_ref[8 + p * Q:8 + (p + 1) * Q, 0:K] = s_ref[p]
+
     pl.semaphore_wait(barrier, len(peers) + len(zpeers))
 
     def rcopy(e, pt, dev, h):
@@ -96,6 +116,13 @@
         return pltpu.make_async_remote_copy(
             src_ref=l_ref, dst_ref=lbuf.at[e - 1],
             send_sem=l_send.at[e - 1], recv_sem=l_recv.at[e - 1], device_id=dev, device_id_type=MESH)
+
+    def lrelay(e):
+        return pltpu.make_async_remote_copy(
+            src_ref=lbuf.at[e - e % U - 1], dst_ref=lbuf.at[e - 1], send_sem=l_send.at[e - 1], recv_sem=l_recv.at[e - 1],
+            device_id={"op": o, "sub": lax.rem(u + e % U, U)}, device_id_type=MESH)
+
+    relayed = [e for e in range(U, T) if e % U]
 
     def up(b, h, e):
         return pltpu.make_async_remote_copy(
@@ -123,8 +150,10 @@
         if h == 0:
             for e, pt, dev in peers:
                 tcopy(e, pt, dev).start()
+    l_in.wait()
     for e, pt, dev in peers:
-        lcopy(e, pt, dev).start()
+        if e < U or e % U == 0:
+            lcopy(e, pt, dev).start()
 
     def gather(h, r):
         if r == 0:
@@ -164,6 +193,7 @@
         return jnp.broadcast_to(tab[:, at:at + 1], (tab.shape[0], N))
 
     def prepare():
+        psi_in.wait()
         for e, pt, dev in peers:
             tcopy(e, pt, dev).wait_recv()
         for e in range(T):
@@ -175,9 +205,17 @@
                     for k in range(K):
                         mask[c, (e * K + k) * LH:(e * K + k + 1) * LH, b * N:(b + 1) * N] = jnp.broadcast_to(hit[k:k + 1], (LH, N)).astype(BF16)
 
+    def relay_left():
+        for e in range(U, T, U):
+            lcopy(e, peers[e - 1][1], peers[e - 1][2]).wait_recv()
+            for f in range(e + 1, e + U):
+                lrelay(f).start()
+
     def prepare_left():
-        for e, pt, dev in peers:
-            lcopy(e, pt, dev).wait_recv()
+        for e in range(1, U):
+            lcopy(e, peers[e - 1][1], peers[e - 1][2]).wait_recv()
+        for e in relayed:
+            lrelay(e).wait_recv()
         for e in range(T):
             want = row(table(e), D)
             for d in range(D):
@@ -203,7 +241,7 @@
                     for q in range(Q):
                         coupled = None
                         for p in range(Q):
-                            weight = row(tab, D + 1 + p * Q + q)[k:k + 1]
+                            weight = jnp.broadcast_to(tab[8 + p * Q + q:9 + p * Q + q, k:k + 1], (1, N))
                             part = routed[at:at + LH, p * N:(p + 1) * N] * weight
                             coupled = part if coupled is None else coupled + part
                         cp[(c * Q + q) * LH:(c * Q + q + 1) * LH, (e * K + k) * N:(e * K + k + 1) * N] = coupled.astype(BF16)
@@ -237,6 +275,8 @@
             gather(step[1], step[2])
         elif kind == "prepare":
             prepare()
+        elif kind == "relay":
+            relay_left()
         elif kind == "left":
             prepare_left()
         elif kind == "compute":
@@ -264,16 +304,20 @@
                     down(z + r, h, e).wait_send()
     for e, pt, dev in peers:
         tcopy(e, pt, dev).wait_send()
-        lcopy(e, pt, dev).wait_send()
+        if e in relayed:
+            lrelay(e).wait_send()
+        else:
+            lcopy(e, pt, dev).wait_send()
 
 
 def steps(Z, H):
     if H == 1:
         order = [("gather", 0, 0), ("prepare",)]
-        order += [("gather", 0, r) for r in range(1, Z - 1)]
+        order += [("gather", 0, 1), ("relay",)]
+        order += [("gather", 0, r) for r in range(2, Z - 1)]
         order += [("left",), ("gather", 0, Z - 1), ("compute", 0), ("products", 0), ("finish", 0)]
         return order
-    order = [("gather", 0, 0), ("prepare",), ("gather", 0, 1), ("gather", 0, 2), ("gather", 1, 0), ("left",)]
+    order = [("gather", 0, 0), ("prepare",), ("gather", 0, 1), ("relay",), ("gather", 0, 2), ("gather", 1, 0), ("left",)]
     order += [("gather", 0, 3), ("gather", 1, 1), ("compute", 0), ("products", 0), ("gather", 1, 2)]
     order += [("gather", 1, 3), ("compute", 1), ("products", 1), ("finish", 0), ("finish", 1)]
     return order
@@ -284,18 +328,24 @@
     _, D, Q, N, _ = wavefunction.shape
     T, H = O * U, PARTS
     LH = N // T // H
-    own = lax.axis_index("sector")
-    left = lax.dynamic_slice_in_dim(left_map, own, 1, axis=1)
-    tab = jnp.concatenate([right_map.astype(F32), left.astype(F32), site_ops.reshape(K, Q * Q)], axis=1)
-    tab = jnp.pad(tab, ((0, -K % 8), (0, 128 - tab.shape[1])))
+    tab = jax.ShapeDtypeStruct((8 + -(-Q * Q // 8) * 8, 128), F32)
+    site = site_ops.transpose(1, 2, 0)
     dma = pltpu.SemaphoreType.DMA
     vmem = pl.BlockSpec(memory_space=pltpu.VMEM)
+    hbm = pl.BlockSpec(memory_space=pltpu.HBM)
     out = pl.pallas_call(
         functools.partial(fused_kernel, Z, O, U, K, D, Q, N, H, steps(Z, H)),
         out_shape=jax.ShapeDtypeStruct((T, H, Q, LH, N), BF16),
-        in_specs=[vmem] * 4,
+        in_specs=[hbm] * 6,
         out_specs=vmem,
         scratch_shapes=[
+            pltpu.VMEM(wavefunction.shape, BF16),
+            pltpu.VMEM(right_env.shape, BF16),
+            pltpu.VMEM(left_env.shape, BF16),
+            pltpu.VMEM(site.shape, F32),
+            pltpu.VMEM(right_map.shape, jnp.int32),
+            pltpu.VMEM(left_map.shape, jnp.int32),
+            pltpu.VMEM(tab.shape, F32),
             pltpu.VMEM((T, H, K, LH, N), BF16),
             pltpu.VMEM((D, H, T, K, LH, N), BF16),
             pltpu.VMEM((T - 1,) + left_env.shape, BF16),
@@ -307,13 +357,13 @@
             pltpu.VMEM((H, D, Q * LH, D * N), BF16),
             pltpu.VMEM((H, D, Q * LH, D * N), BF16),
             pltpu.VMEM((H, D, Q, LH, N), BF16),
-            dma((H, T)), dma((D, H, T)), dma((D, H, T)), dma((D, H, T)),
+            dma((6,)), dma((H, T)), dma((D, H, T)), dma((D, H, T)), dma((D, H, T)),
             dma((T - 1,)), dma((T - 1,)), dma((T - 1,)), dma((T - 1,)),
             dma((H, Z - 1)), dma((H, Z)), dma((H, T - 1)), dma((H, T - 1)),
         ],
-        compiler_params=pltpu.CompilerParams(collective_id=0, has_side_effects=True, vmem_limit_bytes=40 << 20),
+        compiler_params=pltpu.CompilerParams(collective_id=0, has_side_effects=True, vmem_limit_bytes=60 << 20),
         name="sigma",
-    )(wavefunction, right_env, left_env, tab)
+    )(wavefunction, right_env, left_env, site, right_map, left_map)
     out = out.transpose(2, 4, 0, 1, 3).reshape(1, 1, Q, N, N)
     return out
 
@@ -327,7 +377,7 @@
         a, D, Q, N, _ = wavefunction.shape
         T = O * U
         small = T * K * D * N * N * 2 <= (8 << 20)
-        if small and a == 1 and D == Z and D == T and N % (16 * T * PARTS) == 0 and N == 128:
+        if small and a == 1 and D == Z and D == T and Z > 2 and K <= 8 and N % (16 * T * PARTS) == 0 and N == 128:
             return fused_plan(Z, O, U, wavefunction, right_env, left_env, site_ops, right_map, left_map)
         return routed_plan(wavefunction, right_env, left_env, site_ops, right_map, left_map)
 

time: 34.8 us -> 31.3 us (0.90)
  local copies, waits for them, and re-layouts: 5.48 us -> 1.59 us
  Pallas kernels: 28.9 us -> 29.6 us
    unnamed x12 -> x0, local copies, waits for them, and re-layouts: 4.64 us -> none
    transpose x1, local copies, waits for them, and re-layouts: 0.01 us -> 0.85 us  [fused_plan(): out = out.transpose(2, 4, 0, 1, 3).reshape(1, 1, Q, N, N)]
    pallas_call x1, Pallas kernels: 28.9 us -> 29.6 us  [fused_plan(): pl.pallas_call(functools.partial(fused_kernel, Z, O, U, K, D, Q, N, H, st...]
where the time goes in v2:
time: 31.3 us; the launch traced here: 31.2 us
  Pallas kernels  29.6 us (95%)
  local copies, waits for them, and re-layouts  1.59 us (5%)
    pallas_call x1, Pallas kernels, fused_plan(): pl.pallas_call(functools.partial(fused_kernel, Z, O, U, K, D, Q, N, H, st...  29.6 us
    transpose x1, local copies, waits for them, and re-layouts, fused_plan(): out = out.transpose(2, 4, 0, 1, 3).reshape(1, 1, Q, N, N)  0.85 us
    reshape x1, local copies, waits for them, and re-layouts, fused_plan(): out = out.transpose(2, 4, 0, 1, 3).reshape(1, 1, Q, N, N)  0.74 us

profile of v2, /device:TPU:0, one launch (start us, length us, event | category | flops | bytes accessed | tf_op | source)
XLA Modules:
  0.0 31.2 jit_solution(12237321136771961833)
XLA Ops:
  0.0 29.6 %sigma.1 = bf16[4,1,2,32,128]{4,3,2,1,0:T(8,128)(2,1)} custom-call(bf16[1,4,2,128,128]{4,3,2,1,0:T(8,128)(2,1)} %psi_hbm.1, bf16[4,1,128,128]{3,2,1,0:T(8,128)(2,1)} %r_hbm.1, bf16[4,1,128,128]{3,2,1,0:T(8,128)(2,1)} %l_hbm.1, f32[2,2,4]{2,1,0:T(2,128)} %bitcast.5, s32[4,4]{1,0:T(4,128)} %rm_hbm.1, s32[4,4]{1,0:T(4,128)} %lm_hbm.1), custom_call_target="tpu_custom_call" | custom-call | tf_op jit(solution)/shard_map/sigma/pallas_call | solution.py:336
  29.6 0.8 %copy.7 = bf16[2,128,4,1,32]{1,4,2,0,3:T(8,128)(2,1)S(1)} copy(bf16[2,128,4,1,32]{1,4,0,3,2:T(8,128)(2,1)} %bitcast.3) | data formatting | bytes 131072 | tf_op jit(solution)/shard_map/transpose | solution.py:367
  30.4 0.7 %copy.8 = bf16[1,1,2,128,128]{4,3,2,1,0:T(8,128)(2,1)} copy(bf16[1,1,2,128,128]{3,4,2,1,0:T(8,128)(2,1)S(1)} %bitcast.4) | data formatting | bytes 131072 | tf_op jit(solution)/shard_map/reshape | solution.py:367

commit v3 on v2

--- a/solution.py
+++ b/solution.py
@@ -77,8 +77,10 @@
     barrier = pltpu.get_barrier_semaphore()
     for e, pt, dev in peers:
         pl.semaphore_signal(barrier, inc=1, device_id=dev, device_id_type=MESH)
-    for r, pz in zpeers:
-        pl.semaphore_signal(barrier, inc=1, device_id={"sector": pz}, device_id_type=MESH)
+    for near, there in ((z + 1, z < Z - 1), (z - 1, z > 0)):
+        @pl.when(there)
+        def _():
+            pl.semaphore_signal(barrier, inc=1, device_id={"sector": near}, device_id_type=MESH)
 
     r_in.wait()
     for k in range(K):
@@ -100,7 +102,7 @@
     for p in range(Q):
         tab_ref[8 + p * Q:8 + (p + 1) * Q, 0:K] = s_ref[p]
 
-    pl.semaphore_wait(barrier, len(peers) + len(zpeers))
+    pl.semaphore_wait(barrier, len(peers) + jnp.where(z < Z - 1, 1, 0) + jnp.where(z > 0, 1, 0))
 
     def rcopy(e, pt, dev, h):
         return pltpu.make_async_remote_copy(
@@ -141,7 +143,7 @@
 
     def fcopy(h, e, pt, dev):
         return pltpu.make_async_remote_copy(
-            src_ref=fin.at[h, pt], dst_ref=out_ref.at[t, h],
+            src_ref=fin.at[h, pt], dst_ref=out_ref.at[:, t, h],
             send_sem=f_send.at[h, e - 1], recv_sem=f_recv.at[h, e - 1], device_id=dev, device_id_type=MESH)
 
     for h in range(H):
@@ -150,10 +152,6 @@
         if h == 0:
             for e, pt, dev in peers:
                 tcopy(e, pt, dev).start()
-    l_in.wait()
-    for e, pt, dev in peers:
-        if e < U or e % U == 0:
-            lcopy(e, pt, dev).start()
 
     def gather(h, r):
         if r == 0:
@@ -204,6 +202,12 @@
                     hit = jnp.where(want == float(c), 1.0, 0.0)
                     for k in range(K):
                         mask[c, (e * K + k) * LH:(e * K + k + 1) * LH, b * N:(b + 1) * N] = jnp.broadcast_to(hit[k:k + 1], (LH, N)).astype(BF16)
+
+    def send_left():
+        l_in.wait()
+        for e, pt, dev in peers:
+            if e < U or e % U == 0:
+                lcopy(e, pt, dev).start()
 
     def relay_left():
         for e in range(U, T, U):
@@ -267,7 +271,7 @@
             fin[h, d] = total[:, d * N:(d + 1) * N].reshape(Q, LH, N)
         for e, pt, dev in peers:
             fcopy(h, e, pt, dev).start()
-        out_ref[t, h] = fin[h, t]
+        out_ref[:, t, h] = fin[h, t]
 
     for step in order:
         kind = step[0]
@@ -275,6 +279,8 @@
             gather(step[1], step[2])
         elif kind == "prepare":
             prepare()
+        elif kind == "send":
+            send_left()
         elif kind == "relay":
             relay_left()
         elif kind == "left":
@@ -312,7 +318,7 @@
 
 def steps(Z, H):
     if H == 1:
-        order = [("gather", 0, 0), ("prepare",)]
+        order = [("gather", 0, 0), ("send",), ("prepare",)]
         order += [("gather", 0, 1), ("relay",)]
         order += [("gather", 0, r) for r in range(2, Z - 1)]
         order += [("left",), ("gather", 0, Z - 1), ("compute", 0), ("products", 0), ("finish", 0)]
@@ -335,7 +341,7 @@
     hbm = pl.BlockSpec(memory_space=pltpu.HBM)
     out = pl.pallas_call(
         functools.partial(fused_kernel, Z, O, U, K, D, Q, N, H, steps(Z, H)),
-        out_shape=jax.ShapeDtypeStruct((T, H, Q, LH, N), BF16),
+        out_shape=jax.ShapeDtypeStruct((Q, T, H, LH, N), BF16),
         in_specs=[hbm] * 6,
         out_specs=vmem,
         scratch_shapes=[
@@ -364,8 +370,7 @@
         compiler_params=pltpu.CompilerParams(collective_id=0, has_side_effects=True, vmem_limit_bytes=60 << 20),
         name="sigma",
     )(wavefunction, right_env, left_env, site, right_map, left_map)
-    out = out.transpose(2, 4, 0, 1, 3).reshape(1, 1, Q, N, N)
-    return out
+    return out.reshape(1, 1, Q, N, N).swapaxes(3, 4)
 
 
 def solution(mesh):

time: 31.3 us -> 30.7 us (0.981)
  Pallas kernels: 29.6 us -> 28.9 us
    transpose x1 -> x0, local copies, waits for them, and re-layouts: 0.85 us -> none  [fused_plan(): out = out.transpose(2, 4, 0, 1, 3).reshape(1, 1, Q, N, N)]
    reshape x1, local copies, waits for them, and re-layouts: 0.74 us -> 1.57 us  [fused_plan(): return out.reshape(1, 1, Q, N, N).swapaxes(3, 4)]
    pallas_call x1, Pallas kernels: 29.6 us -> 28.9 us  [fused_plan(): pl.pallas_call(functools.partial(fused_kernel, Z, O, U, K, D, Q, N, H, st...]
where the time goes in v3:
time: 30.7 us; the launch traced here: 30.5 us
  Pallas kernels  28.9 us (94%)
  local copies, waits for them, and re-layouts  1.57 us (5%)
    pallas_call x1, Pallas kernels, fused_plan(): pl.pallas_call(functools.partial(fused_kernel, Z, O, U, K, D, Q, N, H, st...  28.9 us
    reshape x1, local copies, waits for them, and re-layouts, fused_plan(): return out.reshape(1, 1, Q, N, N).swapaxes(3, 4)  1.57 us

profile of v3, /device:TPU:0, one launch (start us, length us, event | category | flops | bytes accessed | tf_op | source)
XLA Modules:
  0.0 30.5 jit_solution(6330929151955948743)
XLA Ops:
  0.0 28.9 %sigma.1 = bf16[2,4,1,32,128]{4,3,2,1,0:T(8,128)(2,1)} custom-call(bf16[1,4,2,128,128]{4,3,2,1,0:T(8,128)(2,1)} %psi_hbm.1, bf16[4,1,128,128]{3,2,1,0:T(8,128)(2,1)} %r_hbm.1, bf16[4,1,128,128]{3,2,1,0:T(8,128)(2,1)} %l_hbm.1, f32[2,2,4]{2,1,0:T(2,128)} %bitcast.4, s32[4,4]{1,0:T(4,128)} %rm_hbm.1, s32[4,4]{1,0:T(4,128)} %lm_hbm.1), custom_call_target="tpu_custom_call" | custom-call | tf_op jit(solution)/shard_map/sigma/pallas_call | solution.py:342
  28.9 1.6 %copy.7 = bf16[1,1,2,128,128]{3,4,2,1,0:T(8,128)(2,1)} copy(bf16[1,1,2,128,128]{4,3,2,1,0:T(8,128)(2,1)} %bitcast.3) | data formatting | bytes 131072 | tf_op jit(solution)/shard_map/reshape | solution.py:373

commit v4 on v3

--- a/solution.py
+++ b/solution.py
@@ -256,7 +256,7 @@
             part = sums[c * Q * LH:(c + 1) * Q * LH]
             pf[h, c] = part
             psend[h, c] = part.astype(BF16)
-        for r, pz in zpeers[::-1]:
+        for r, pz in zpeers:
             pcopy(h, r, pz).start()
 
     def finish(h):

time: 30.7 us -> 29.3 us (0.954)
  Pallas kernels: 28.9 us -> 27.6 us
    pallas_call x1, Pallas kernels: 28.9 us -> 27.6 us  [fused_plan(): pl.pallas_call(functools.partial(fused_kernel, Z, O, U, K, D, Q, N, H, st...]
where the time goes in v4:
time: 29.3 us; the launch traced here: 29.2 us
  Pallas kernels  27.6 us (94%)
  local copies, waits for them, and re-layouts  1.57 us (5%)
    pallas_call x1, Pallas kernels, fused_plan(): pl.pallas_call(functools.partial(fused_kernel, Z, O, U, K, D, Q, N, H, st...  27.6 us
    reshape x1, local copies, waits for them, and re-layouts, fused_plan(): return out.reshape(1, 1, Q, N, N).swapaxes(3, 4)  1.57 us

profile of v4, /device:TPU:0, one launch (start us, length us, event | category | flops | bytes accessed | tf_op | source)
XLA Modules:
  0.0 29.2 jit_solution(16911812876713082849)
XLA Ops:
  0.0 27.6 %sigma.1 = bf16[2,4,1,32,128]{4,3,2,1,0:T(8,128)(2,1)} custom-call(bf16[1,4,2,128,128]{4,3,2,1,0:T(8,128)(2,1)} %psi_hbm.1, bf16[4,1,128,128]{3,2,1,0:T(8,128)(2,1)} %r_hbm.1, bf16[4,1,128,128]{3,2,1,0:T(8,128)(2,1)} %l_hbm.1, f32[2,2,4]{2,1,0:T(2,128)} %bitcast.4, s32[4,4]{1,0:T(4,128)} %rm_hbm.1, s32[4,4]{1,0:T(4,128)} %lm_hbm.1), custom_call_target="tpu_custom_call" | custom-call | tf_op jit(solution)/shard_map/sigma/pallas_call | solution.py:342
  27.6 1.6 %copy.7 = bf16[1,1,2,128,128]{3,4,2,1,0:T(8,128)(2,1)} copy(bf16[1,1,2,128,128]{4,3,2,1,0:T(8,128)(2,1)} %bitcast.3) | data formatting | bytes 131072 | tf_op jit(solution)/shard_map/reshape | solution.py:373
